TPU v7x, 256 devices: a whole 4x4x8 slice. The times are simulated.
256 devices in a mesh: rows: 16 (over y, z_hi, core), bricks: 16 (over x, z_lo).
Axes of the slice: x: 4, y: 4, z: 8 (z_hi: 2, z_lo: 4; z = z_hi * 4 + z_lo), core: 2. Of those that a mesh axis runs over, the one named last changes fastest.
Arguments:
- load: float32 [16, 16, 576], P('rows', 'bricks'), may hold values from -12 to 12
- stiffness: float32 [16, 16, 576, 576], P('rows', 'bricks'), may hold values from -1 to 10, as said below
- local_inverse: float32 [16, 16, 576, 576], P('rows', 'bricks'), may hold values from -1 to 4, as said below
- intact: int32 [16, 16, 96, 96], P('rows', 'bricks'), may hold values from 0 to 1, as said below
- face_lists: int32 [16, 16, 4, 24], P('rows', 'bricks'), may hold values from 0 to 95, as said below
- coarse_basis: float32 [16, 16, 64, 576], P('rows', 'bricks'), may hold values from -0.25 to 0.25
- coarse_matrix: float32 [16, 16, 16, 64, 64], P('rows', 'bricks'), may hold values from -1 to 10, as said below
- coarse_pattern: int32 [16, 16, 16], P('rows', 'bricks'), may hold values from 0 to 1, as said below
Outputs:
- solution: float32 [16, 16, 576], P('rows', 'bricks')
- residual: float32 [16, 16, 576], P('rows', 'bricks')
Inputs may be any that keep to these rules, and one draw needn't show every extreme that they name: stiffness[r, b] is symmetric positive definite, and stays so with any symmetric set of its off-diagonal node blocks zeroed. local_inverse[r, b] is symmetric positive definite. intact[r, b] is symmetric in its two node indices, with ones on the diagonal. `face_lists`: each list of 24 node numbers holds distinct numbers. `coarse_matrix`: for each r, block (i, j) of the coarse operator is exactly the transpose of block (j, i); the whole is positive definite, and stays so with any symmetric set of off-diagonal blocks dropped. coarse_pattern[r] is symmetric in its two brick indices, with ones on the diagonal.
All inputs are finite; a program needn't handle non-finite values.
Results may differ from a plain program's by a relative error of at most 0.0003.
Values sent between devices are 32-bit elements; how exact they have to be, the bound alone decides.
A program may use at most 128 MiB of HBM per device.

v0:
```python
import functools

import jax
import jax.numpy as jnp
from jax import lax
from jax.experimental import pallas as pl
from jax.experimental.pallas import tpu as pltpu
from jax.sharding import PartitionSpec as P

MESH = pl.DeviceIdType.MESH
HI = lax.Precision.HIGHEST
F32 = jnp.float32
NODES, NDOF, COARSE, FACE, W = 96, 576, 64, 24, 128
LANES = 128


def dot(a, b, dims=((1,), (0,))):
    return lax.dot_general(a, b, (dims, ((), ())), precision=HI, preferred_element_type=F32)


def small_product(a, b):
    out = []
    for row in a:
        line = []
        for j in range(len(b[0])):
            acc = row[0] * b[0][j]
            for k in range(1, len(b)):
                acc = acc + row[k] * b[k][j]
            line.append(acc)
        out.append(line)
    return out


def small_inverse(m):
    n = len(m)
    if n == 2:
        a, b, d = m[0][0], m[0][1], m[1][1]
        r = 1.0 / (a * d - b * b)
        off = -(b * r)
        return [[d * r, off], [off, a * r]]
    h = n // 2
    b = [row[h:] for row in m[:h]]
    e = small_inverse([row[:h] for row in m[:h]])
    w = small_product(e, b)
    s = [[None] * h for _ in range(h)]
    for i in range(h):
        for j in range(i, h):
            acc = b[0][i] * w[0][j]
            for k in range(1, h):
                acc = acc + b[k][i] * w[k][j]
            s[i][j] = s[j][i] = m[h + i][h + j] - acc
    t = small_inverse(s)
    x = small_product(w, t)
    top = [[None] * h for _ in range(h)]
    for i in range(h):
        for j in range(i, h):
            acc = x[i][0] * w[j][0]
            for k in range(1, h):
                acc = acc + x[i][k] * w[j][k]
            top[i][j] = top[j][i] = e[i][j] + acc
    neg = [[-v for v in row] for row in x]
    out = [top[i] + neg[i] for i in range(h)]
    out += [[neg[k][i] for k in range(h)] + t[i] for i in range(h)]
    return out


def pivot_groups(count, v):
    shape = (8, LANES)
    sub = lax.broadcasted_iota(jnp.int32, shape, 0)
    lane = lax.broadcasted_iota(jnp.int32, shape, 1)
    v = list(v)
    for g in range(count):
        p = 8 * g
        x = v[g]
        turn = LANES - 8 * count if g == count - 1 else 0
        rows = [jnp.broadcast_to(x[i : i + 1, :], shape) for i in range(8)]
        cols = [jnp.broadcast_to(x[:, p + t : p + t + 1], shape) for t in range(8)]
        m = [[None] * 8 for _ in range(8)]
        for i in range(8):
            for j in range(i, 8):
                m[i][j] = m[j][i] = jnp.broadcast_to(cols[j][i : i + 1, :], shape)
        e = small_inverse(m)
        pivots = (lane >= p) & (lane < p + 8)
        r = [jnp.where(pivots, (lane == p + i).astype(F32), rows[i]) for i in range(8)]
        q = []
        for i in range(8):
            acc = e[i][0] * r[0]
            for j in range(1, 8):
                acc = acc + e[i][j] * r[j]
            q.append(acc)
        new = []
        for k in range(len(v)):
            y = v[k]
            if k == g:
                y = q[0]
                for t in range(1, 8):
                    y = jnp.where(sub == t, q[t], y)
            else:
                acc = jnp.broadcast_to(y[:, p : p + 1], shape) * q[0]
                for t in range(1, 8):
                    acc = acc + jnp.broadcast_to(y[:, p + t : p + t + 1], shape) * q[t]
                y = jnp.where(pivots, 0.0, y) - acc
            new.append(pltpu.roll(y, turn, 1) if turn else y)
        v = new
    return tuple(v[count:] + v[:count])


RUN = 4


class Spread:
    def __init__(self, nb, r, b, all_ref, sems):
        self.nb, self.tiles, self.nx = nb, nb // 2, nb // RUN
        self.r, self.b, self.x, self.z = r, b, lax.div(b, RUN), lax.rem(b, RUN)
        self.all_ref = all_ref
        self.send1, self.recv1, self.send2, self.recv2, self.send3, self.recv3 = sems

    def slot(self, j, brick, count):
        start = pl.multiple_of(brick * COARSE, COARSE)
        return self.all_ref.at[j, pl.ds(start, count * COARSE), :]

    def remote(self, part, send_sem, recv_sem, x, z):
        return pltpu.make_async_remote_copy(
            src_ref=part, dst_ref=part, send_sem=send_sem, recv_sem=recv_sem,
            device_id=(self.r, x * RUN + z), device_id_type=MESH,
        )

    def arrived(self, j, brick, count, sem):
        part = self.slot(j, brick, count)
        pltpu.make_async_copy(part, part, sem).wait()

    def either(self, j, odd, even):
        if isinstance(j, int):
            (odd if j % 2 else even)()
        else:
            pl.when(lax.rem(j, 2) == 1)(odd)
            pl.when(lax.rem(j, 2) == 0)(even)

    def each1(self, j, act):
        part = self.slot(j, self.b, 1)

        def odd():
            for t in range(1, RUN):
                z = lax.rem(self.z + t, RUN)
                act(self.remote(part, self.send1.at[j, t], self.recv1.at[j, self.z], self.x, z))

        def even():
            for t in range(1, self.nx):
                x = lax.rem(self.x + t, self.nx)
                act(self.remote(part, self.send1.at[j, t], self.recv1.at[j, self.x], x, self.z))

        @pl.when(lax.div(self.b, 2) <= j)
        def _():
            self.either(j, odd, even)

    def each2(self, j, act, wait):
        def odd():
            for z in range(RUN):

                @pl.when((self.z != z) & (2 * self.x + z // 2 <= j))
                def _():
                    if wait:
                        self.arrived(j, self.x * RUN + z, 1, self.recv1.at[j, z])

            for count, when in ((RUN, 2 * self.x + 1 <= j), (2, 2 * self.x == j)):

                @pl.when(when)
                def _():
                    part = self.slot(j, self.x * RUN, count)
                    for t in range(1, self.nx):
                        x = lax.rem(self.x + t, self.nx)
                        act(self.remote(part, self.send2.at[j, t], self.recv2.at[j, self.x], x, self.z))

        def even():
            h = j // 2 if isinstance(j, int) else lax.div(j, 2)
            for x in range(self.nx):

                @pl.when(2 * x + lax.div(self.z, 2) <= j)
                def _():
                    brick = x * RUN + self.z
                    if wait:

                        @pl.when(self.x != x)
                        def _():
                            self.arrived(j, brick, 1, self.recv1.at[j, x])

                    for t in range(1, RUN):
                        z = lax.rem(self.z + t, RUN)
                        part = self.slot(j, brick, 1)
                        act(self.remote(part, self.send3.at[h, x, t], self.recv3.at[h, x, self.z], self.x, z))

        self.either(j, odd, even)

    def first(self, j):
        self.each1(j, lambda copy: copy.start())

    def second(self, j):
        self.each2(j, lambda copy: copy.start(), True)

    def need(self, j):
        def odd():
            for x in range(self.nx):
                for count, when in ((RUN, 2 * x + 1 <= j), (2, 2 * x == j)):

                    @pl.when((self.x != x) & when)
                    def _():
                        self.arrived(j, x * RUN, count, self.recv2.at[j, x])

        def even():
            h = j // 2 if isinstance(j, int) else lax.div(j, 2)
            for x in range(self.nx):
                for z in range(RUN):

                    @pl.when((self.z != z) & (2 * x + z // 2 <= j))
                    def _():
                        self.arrived(j, x * RUN + z, 1, self.recv3.at[h, x, z])

        self.either(j, odd, even)

    def finish(self):
        for j in range(self.tiles):
            self.each1(j, lambda copy: copy.wait_send())
            self.each2(j, lambda copy: copy.wait_send(), False)


def factor(nb, b, spread, all_ref, inverse_ref, u_ref, r_ref, l_ref, y_ref, z_ref, p_ref, d_ref):
    tiles = nb // 2
    sub = lax.broadcasted_iota(jnp.int32, (COARSE, W), 0)
    lane = lax.broadcasted_iota(jnp.int32, (COARSE, W), 1)
    half = tiles // 2
    unroll = 2
    turns = W // 8 // unroll

    def tile(k):
        return pl.ds(pl.multiple_of(k * W, W), W)

    def plain(it, v):
        return pivot_groups(unroll, v)

    def with_product(j, depth):
        def run(i, v):
            u = all_ref[j, tile(i), :] - dot(l_ref[i, :, :depth], u_ref[j, :depth, :])
            before = jnp.maximum(i - 1, 0)
            scaled = dot(p_ref[before], u_ref[j, tile(before), :])
            u_ref[j, tile(i), :] = u
            r_ref[j, tile(before), :] = scaled
            l_ref[j, :, tile(before)] = scaled.T
            return pivot_groups(unroll, v)

        return run

    def step(k, far, column):
        depth = (tiles - 1 if far else half) * W
        v = tuple(d_ref[8 * i : 8 * i + 8, :] for i in range(W // 8))
        if column:
            j = k + 1

            @pl.when(k + 5 < tiles)
            def _():
                spread.first(k + 5)

            @pl.when(k + 3 < tiles)
            def _():
                spread.second(k + 3)

            v = lax.fori_loop(0, turns - j, plain, v)
            spread.need(j)
            v = lax.fori_loop(0, half if far else j, with_product(j, (half - 1) * W), v)
            if far:
                v = lax.fori_loop(half, j, with_product(j, (tiles - 2) * W), v)
        else:
            v = lax.fori_loop(0, turns, plain, v)
        inverse = jnp.concatenate(v, axis=0)
        p_ref[k] = inverse
        if column:
            scaled = dot(inverse, u_ref[j, tile(k), :])
            r_ref[j, tile(k), :] = scaled
            l_ref[j, :, tile(k)] = scaled.T
            d_ref[...] = all_ref[j, tile(j), :] - dot(l_ref[j, :, :depth], u_ref[j, :depth, :])
        own = (lane + k * W == sub + b * COARSE).astype(F32)
        own = own - dot(y_ref[:, :depth], r_ref[k, :depth, :])
        y_ref[:, tile(k)] = own
        z_ref[k] = dot(own, inverse)

    def near_step(k, carry):
        step(k, False, True)
        return carry

    def far_step(k, carry):
        step(k, True, True)
        return carry

    spread.need(0)
    d_ref[...] = all_ref[0, :W, :]
    lax.fori_loop(0, half, near_step, 0)
    lax.fori_loop(half, tiles - 1, far_step, 0)
    step(tiles - 1, True, False)
    solved = [None] * tiles
    low = lane < COARSE
    for k in reversed(range(tiles)):
        acc = z_ref[k]
        for j in range(k + 1, tiles):
            acc = acc - dot(solved[j], l_ref[j, :, k * W : k * W + W])
        solved[k] = acc
        inverse_ref[2 * k] = jnp.where(low, acc, 0.0)
        inverse_ref[2 * k + 1] = jnp.where(low, pltpu.roll(acc, COARSE, 1), 0.0)


def whole_kernel(
    nr, nb, pattern_in, matrix_in, load_in, stiffness_in, local_in, intact_in, lists_in, basis_in,
    out_ref, pattern_ref, matrix_ref, load_ref, stiffness_ref, local_ref, intact_ref, lists_ref, basis_ref, in_sem, all_ref, inverse_ref, u_ref, r_ref, l_ref, y_ref, zf_ref, p_ref, d_ref,
    k_ref, m_ref, c_ref, ct_ref, sel_ref, selt_ref, col_ref, z_ref, w_ref, acc_ref,
    msg_ref, gather_ref, tot_ref, total_ref, face_ref, near_ref, send1, recv1, send2, recv2, send3, recv3,
    gather_send, gather_recv, total_send, total_recv, face_send, face_recv,
):
    r, b = lax.axis_index("rows"), lax.axis_index("bricks")
    tiles = nb // 2
    incoming = [
        pltpu.make_async_copy(src, dst, in_sem.at[i])
        for i, (src, dst) in enumerate(
            (
                (pattern_in, pattern_ref), (matrix_in, matrix_ref), (load_in, load_ref), (basis_in, basis_ref),
                (lists_in, lists_ref), (intact_in, intact_ref), (local_in, local_ref), (stiffness_in, stiffness_ref),
            )
        )
    ]
    for copy in incoming:
        copy.start()
    barrier = pltpu.get_barrier_semaphore()
    for t in range(1, nb):
        pl.semaphore_signal(
            barrier, inc=1, device_id=(r, lax.rem(b + t, nb)), device_id_type=MESH
        )
    for t in range(1, nr):
        pl.semaphore_signal(
            barrier, inc=1, device_id=(lax.rem(r + t, nr), b), device_id_type=MESH
        )
    mine = pl.ds(pl.multiple_of(b * COARSE, COARSE), COARSE)
    incoming[0].wait()
    incoming[1].wait()
    for j in range(tiles):
        left = matrix_ref[2 * j] * pattern_ref[0, 2 * j].astype(F32)
        right = matrix_ref[2 * j + 1] * pattern_ref[0, 2 * j + 1].astype(F32)
        all_ref[j, mine, :] = jnp.concatenate([left, right], axis=1)
    spread = Spread(nb, r, b, all_ref, (send1, recv1, send2, recv2, send3, recv3))
    pl.semaphore_wait(barrier, nb + nr - 2)
    for j in range(3):
        spread.first(j)
    for copy in incoming[2:]:
        copy.wait()
    lane8 = lax.broadcasted_iota(jnp.int32, (8, LANES), 1)
    lane1 = lax.broadcasted_iota(jnp.int32, (1, LANES), 1)
    gap = jnp.zeros((NDOF, LANES - NODES), F32)
    for e in range(6):
        span = slice(e * NODES, e * NODES + NODES)
        piece = jnp.concatenate([basis_ref[:, span], gap[:COARSE]], axis=1)
        c_ref[e] = piece
        turned = jnp.concatenate([piece, jnp.zeros((LANES - COARSE, LANES), F32)], axis=0).T
        ct_ref[span, :] = turned[:NODES]
    node_col = lax.broadcasted_iota(jnp.int32, (LANES, LANES), 0)
    node_row = lax.broadcasted_iota(jnp.int32, (LANES, LANES), 1)
    slots = jnp.full((1, LANES), -1, jnp.int32)
    swapped = slots
    for d in range(4):
        line = jnp.concatenate([lists_ref[d : d + 1, :], jnp.zeros((1, LANES - FACE), jnp.int32)], axis=1)
        for other in (False, True):
            at = 32 * (d ^ other)
            moved = pltpu.roll(line, at, 1) if at else line
            here = (lane1 >= at) & (lane1 < at + FACE)
            if other:
                swapped = jnp.where(here, moved, swapped)
            else:
                slots = jnp.where(here, moved, slots)
    sel_ref[:, :LANES] = (node_col == slots).astype(F32)
    sel_ref[:, LANES:] = (node_col == swapped).astype(F32)
    selt_ref[...] = sel_ref[:NODES, :LANES]
    eye = (node_col == node_row)[:NODES]

    def row_to_col(row, ref):
        for c in range(6):
            spread = jnp.where(eye, jnp.broadcast_to(row[c : c + 1, :], (NODES, LANES)), 0.0)
            ref[c * NODES : c * NODES + NODES, :] = jnp.broadcast_to(
                jnp.sum(spread, axis=1, keepdims=True), (NODES, LANES)
            )

    def stack(rows):
        return jnp.concatenate(rows + [jnp.zeros((8 - len(rows), LANES), F32)], axis=0)

    def col_to_row(ref):
        return stack(
            [
                jnp.sum(jnp.where(eye, ref[c * NODES : c * NODES + NODES, :], 0.0), axis=0, keepdims=True)
                for c in range(6)
            ]
        )

    def row_partners(t):
        return (r, lax.rem(b + t, nb))

    def col_partners(t):
        return (lax.rem(r + t, nr), b)

    def exchange(count, partners, msg, land, send_sem, recv_sem):
        for t in range(1, count):
            pltpu.make_async_remote_copy(
                src_ref=msg, dst_ref=land, send_sem=send_sem, recv_sem=recv_sem,
                device_id=partners(t), device_id_type=MESH,
            ).start()

    def wait_bytes(ref, sem):
        pltpu.make_async_copy(ref, ref, sem).wait()

    def gather_start(n, message):
        msg_ref[n] = message
        gather_ref[n, b] = message
        exchange(
            nb, row_partners, msg_ref.at[n], gather_ref.at[n, b], gather_send.at[n], gather_recv.at[n]
        )

    def gather_wait(n):
        wait_bytes(gather_ref.at[n, pl.ds(0, nb - 1)], gather_recv.at[n])

    def total_start(n):
        acc = gather_ref[n, 0]
        for j in range(1, nb):
            acc = acc + gather_ref[n, j]
        tot_ref[n] = acc
        total_ref[n, r] = acc
        exchange(
            nr, col_partners, tot_ref.at[n], total_ref.at[n, r], total_send.at[n], total_recv.at[n]
        )

    def total_wait(n):
        wait_bytes(total_ref.at[n, pl.ds(0, nr - 1)], total_recv.at[n])
        acc = total_ref[n, 0]
        for j in range(1, nr):
            acc = acc + total_ref[n, j]
        first = jnp.sum(jnp.where(lane1 == COARSE, acc, 0.0), axis=1, keepdims=True)
        second = jnp.sum(jnp.where(lane1 == COARSE + 1, acc, 0.0), axis=1, keepdims=True)
        return first, second

    def reduced(ref):
        return jnp.sum(ref[...] * ct_ref[...], axis=0, keepdims=True)

    def with_dots(message, first, second):
        one = jnp.sum(jnp.sum(first, axis=0, keepdims=True), axis=1, keepdims=True)
        two = jnp.sum(jnp.sum(second, axis=0, keepdims=True), axis=1, keepdims=True)
        message = jnp.where(lane1 == COARSE, one, message)
        return jnp.where(lane1 == COARSE + 1, two, message)

    def local_part(ref):
        return [jnp.sum(ref[...] * m_ref[e], axis=0, keepdims=True) for e in range(6)]

    def coarse_part(n):
        acc = inverse_ref[0] * gather_ref[n, 0]
        for j in range(1, nb):
            acc = acc + inverse_ref[j] * gather_ref[n, j]
        solved = jnp.sum(acc, axis=1, keepdims=True)
        return [jnp.sum(solved * c_ref[e], axis=0, keepdims=True) for e in range(6)]

    neighbours = [
        (lax.rem(r + nr - 1, nr), b, r > 0),
        (lax.rem(r + 1, nr), b, r < nr - 1),
        (r, lax.rem(b + nb - 1, nb), b > 0),
        (r, lax.rem(b + 1, nb), b < nb - 1),
    ]

    def face_start(n, row):
        both = dot(row, sel_ref[...])
        face_ref[n] = both[:, LANES:]
        for d in range(4):
            pltpu.make_async_remote_copy(
                src_ref=face_ref.at[n], dst_ref=near_ref.at[n, d ^ 1],
                send_sem=face_send.at[n, d], recv_sem=face_recv.at[n, d ^ 1],
                device_id=neighbours[d][:2], device_id_type=MESH,
            ).start()
        return both[:, :LANES]

    def operate(n, row, face, target):
        for c in range(6):
            rows = slice(c * NODES, c * NODES + NODES)
            acc = k_ref[0, rows, :] * row[0:1, :]
            for e in range(1, 6):
                acc = acc + k_ref[e, rows, :] * row[e : e + 1, :]
            acc_ref[rows, :] = acc
        stretch = face
        for d in range(4):
            wait_bytes(near_ref.at[n, d], face_recv.at[n, d])
            here = (lane8 >= 32 * d) & (lane8 < 32 * d + 32) & neighbours[d][2]
            stretch = stretch - jnp.where(here, near_ref[n, d], 0.0)
        for c in range(6):
            rows = slice(c * NODES, c * NODES + NODES)
            acc = acc_ref[rows, :] + selt_ref[...] * stretch[c : c + 1, :]
            target[rows, :] = jnp.broadcast_to(
                jnp.sum(acc, axis=1, keepdims=True), (NODES, LANES)
            )

    load = stack([jnp.concatenate([load_ref[:, c * NODES : c * NODES + NODES], gap[:1]], axis=1) for c in range(6)])
    row_to_col(load, col_ref)
    res = load
    gather_start(0, reduced(col_ref))
    for j in range(2):
        spread.second(j)
    spread.first(3)
    for ref in (u_ref, r_ref, l_ref, p_ref):
        for j in range(tiles):
            ref[j] = jnp.zeros(ref.shape[1:], F32)
    y_ref[...] = jnp.zeros(y_ref.shape, F32)
    spread.second(2)
    if tiles > 4:
        spread.first(4)
    intact = intact_ref[...].astype(F32)
    for e in range(6):
        span = slice(e * NODES, e * NODES + NODES)
        part = jnp.concatenate([stiffness_ref[:, span], gap], axis=1)
        mask = jnp.concatenate([intact, gap[:NODES]], axis=1)
        for c in range(6):
            rows = slice(c * NODES, c * NODES + NODES)
            k_ref[e, rows, :] = part[rows] * mask
        m_ref[e] = jnp.concatenate([local_ref[:, span], gap], axis=1)
    part = stack(local_part(col_ref))
    gather_wait(0)

    factor(nb, b, spread, all_ref, inverse_ref, u_ref, r_ref, l_ref, y_ref, zf_ref, p_ref, d_ref)

    u = part + stack(coarse_part(0))
    face = face_start(0, u)
    operate(0, u, face, w_ref)
    w = col_to_row(w_ref)
    p = s = q = sol = None
    dot_old = step_old = None
    for i in range(2):
        gather_start(i + 1, with_dots(reduced(w_ref), res * u, w * u))
        part = local_part(w_ref)
        gather_wait(i + 1)
        total_start(i + 1)
        m = stack([x + y for x, y in zip(part, coarse_part(i + 1))])
        face = face_start(i + 1, m)
        operate(i + 1, m, face, col_ref)
        v = col_to_row(col_ref)
        gamma, delta = total_wait(i + 1)
        if i == 0:
            step_size = gamma / delta
            p, s, q, zr = u, w, m, v
            z_ref[...] = col_ref[...]
            sol = step_size * p
        else:
            ratio = gamma / dot_old
            step_size = gamma / (delta - ratio * gamma / step_old)
            p, s, q, zr = u + ratio * p, w + ratio * s, m + ratio * q, v + ratio * zr
            sol = sol + step_size * p
        res = res - step_size * s
        u = u - step_size * q
        w = w - step_size * zr
        if i == 0:
            w_ref[...] = w_ref[...] - step_size * z_ref[...]
        dot_old, step_old = gamma, step_size
    gather_start(3, with_dots(jnp.zeros((1, LANES), F32), res * u, w * u))
    gather_wait(3)
    total_start(3)
    gamma, delta = total_wait(3)
    ratio = gamma / dot_old
    step_size = gamma / (delta - ratio * gamma / step_old)
    out_ref[0] = sol + step_size * (u + ratio * p)
    out_ref[1] = res - step_size * (w + ratio * s)

    spread.finish()
    for n in range(4):
        wait_bytes(gather_ref.at[n, pl.ds(0, nb - 1)], gather_send.at[n])
    for n in range(1, 4):
        wait_bytes(total_ref.at[n, pl.ds(0, nr - 1)], total_send.at[n])
    for n in range(3):
        for d in range(4):
            wait_bytes(face_ref.at[n], face_send.at[n, d])


VMEM = pl.BlockSpec(memory_space=pltpu.VMEM)
ANY = pl.BlockSpec(memory_space=pltpu.HBM)


def body(nr, nb, load, stiffness, local_inverse, intact, face_lists, coarse_basis, matrix, pattern):
    tiles = nb // 2
    order = nb * COARSE
    limit = 62 * 1024 * 1024
    out = pl.pallas_call(
        functools.partial(whole_kernel, nr, nb),
        out_shape=jax.ShapeDtypeStruct((2, 8, LANES), F32),
        in_specs=[ANY] * 8,
        out_specs=VMEM,
        scratch_shapes=[
            pltpu.SMEM((1, nb), jnp.int32),
            pltpu.VMEM((nb, COARSE, COARSE), F32),
            pltpu.VMEM((1, NDOF), F32),
            pltpu.VMEM((NDOF, NDOF), F32),
            pltpu.VMEM((NDOF, NDOF), F32),
            pltpu.VMEM((NODES, NODES), jnp.int32),
            pltpu.VMEM((4, FACE), jnp.int32),
            pltpu.VMEM((COARSE, NDOF), F32),
            pltpu.SemaphoreType.DMA((8,)),
            pltpu.VMEM((tiles, order, LANES), F32),
            pltpu.VMEM((nb, COARSE, LANES), F32),
            pltpu.VMEM((tiles, order, LANES), F32),
            pltpu.VMEM((tiles, order, LANES), F32),
            pltpu.VMEM((tiles, W, order), F32),
            pltpu.VMEM((COARSE, order), F32),
            pltpu.VMEM((tiles, COARSE, W), F32),
            pltpu.VMEM((tiles, W, W), F32),
            pltpu.VMEM((W, W), F32),
            pltpu.VMEM((6, NDOF, LANES), F32),
            pltpu.VMEM((6, NDOF, LANES), F32),
            pltpu.VMEM((6, COARSE, LANES), F32),
            pltpu.VMEM((NDOF, LANES), F32),
            pltpu.VMEM((LANES, 2 * LANES), F32),
            pltpu.VMEM((NODES, LANES), F32),
            pltpu.VMEM((NDOF, LANES), F32),
            pltpu.VMEM((NDOF, LANES), F32),
            pltpu.VMEM((NDOF, LANES), F32),
            pltpu.VMEM((NDOF, LANES), F32),
            pltpu.VMEM((4, 1, LANES), F32),
            pltpu.VMEM((4, nb, 1, LANES), F32),
            pltpu.VMEM((4, 1, LANES), F32),
            pltpu.VMEM((4, nr, 1, LANES), F32),
            pltpu.VMEM((3, 8, LANES), F32),
            pltpu.VMEM((3, 4, 8, LANES), F32),
            pltpu.SemaphoreType.DMA((tiles, RUN)),
            pltpu.SemaphoreType.DMA((tiles, RUN)),
            pltpu.SemaphoreType.DMA((tiles, nb // RUN)),
            pltpu.SemaphoreType.DMA((tiles, nb // RUN)),
            pltpu.SemaphoreType.DMA((tiles // 2, nb // RUN, RUN)),
            pltpu.SemaphoreType.DMA((tiles // 2, nb // RUN, RUN)),
            pltpu.SemaphoreType.DMA((4,)),
            pltpu.SemaphoreType.DMA((4,)),
            pltpu.SemaphoreType.DMA((4,)),
            pltpu.SemaphoreType.DMA((4,)),
            pltpu.SemaphoreType.DMA((3, 4)),
            pltpu.SemaphoreType.DMA((3, 4)),
        ],
        compiler_params=pltpu.CompilerParams(
            collective_id=0, has_side_effects=True, vmem_limit_bytes=limit
        ),
        name="whole",
    )(
        pattern.reshape(1, nb),
        matrix.reshape(nb, COARSE, COARSE),
        load.reshape(1, NDOF),
        stiffness.reshape(NDOF, NDOF),
        local_inverse.reshape(NDOF, NDOF),
        intact.reshape(NODES, NODES),
        face_lists.reshape(4, FACE),
        coarse_basis.reshape(COARSE, NDOF),
    )
    flat = out[:, :6, :NODES].reshape(2, 1, 1, NDOF)
    return flat[0], flat[1]


def solution(mesh):
    in_specs = (
        P("rows", "bricks", None),
        P("rows", "bricks", None, None),
        P("rows", "bricks", None, None),
        P("rows", "bricks", None, None),
        P("rows", "bricks", None, None),
        P("rows", "bricks", None, None),
        P("rows", "bricks", None, None, None),
        P("rows", "bricks", None),
    )
    out_specs = (P("rows", "bricks", None), P("rows", "bricks", None))
    run = functools.partial(body, mesh.shape["rows"], mesh.shape["bricks"])
    return jax.shard_map(run, mesh=mesh, in_specs=in_specs, out_specs=out_specs, check_vma=False)
```

profile of v0, /device:TPU:1, one launch (start us, length us, event | category | flops | bytes accessed | tf_op | source)
XLA Modules:
  0.0 135.6 jit_solution(2578961552199854169)
XLA Ops:
  0.6 132.9 %whole.1 = f32[2,8,128]{2,1,0:T(8,128)} custom-call(s32[1,16]{1,0:T(1,128)} %bitcast.15, f32[16,64,64]{2,1,0:T(8,128)} %bitcast.10, f32[1,576]{1,0:T(1,128)} %bitcast.13, f32[576,576]{1,0:T(8,128)} %bitcast.8, f32[576,576]{1,0:T(8,128)} %bitcast.9, s32[96,96]{1,0:T(8,128)} %bitcast.12, s32[4,24]{1,0:T(4,128)} %bitcast.14, f32[64,576]{1,0:T(8,128)} %bitcast.11), custom_call_target="tpu_custom_call" | custom-call | tf_op jit(solution)/shard_map/whole/pallas_call | solution.py:585
  133.6 0.7 fusion
  134.2 0.7 squeeze.7
  134.9 0.7 squeeze.6
where the time goes:
time: 136 us
  Pallas kernels  133 us (98%)
  local copies, waits for them, and re-layouts  1.99 us (1%)
    pallas_call x1, Pallas kernels, body(): pl.pallas_call(functools.partial(whole_kernel, nr, nb), out_shape=jax.Sha...  133 us

commit v1 on v0

--- a/solution.py
+++ b/solution.py
@@ -9,13 +9,16 @@
 
 MESH = pl.DeviceIdType.MESH
 HI = lax.Precision.HIGHEST
+MID = lax.Precision.HIGH
 F32 = jnp.float32
 NODES, NDOF, COARSE, FACE, W = 96, 576, 64, 24, 128
 LANES = 128
 
 
-def dot(a, b, dims=((1,), (0,))):
-    return lax.dot_general(a, b, (dims, ((), ())), precision=HI, preferred_element_type=F32)
+def dot(a, b, precision=HI):
+    return lax.dot_general(
+        a, b, (((1,), (0,)), ((), ())), precision=precision, preferred_element_type=F32
+    )
 
 
 def small_product(a, b):
@@ -239,9 +242,9 @@
 
     def with_product(j, depth):
         def run(i, v):
-            u = all_ref[j, tile(i), :] - dot(l_ref[i, :, :depth], u_ref[j, :depth, :])
+            u = all_ref[j, tile(i), :] - dot(l_ref[i, :, :depth], u_ref[j, :depth, :], MID)
             before = jnp.maximum(i - 1, 0)
-            scaled = dot(p_ref[before], u_ref[j, tile(before), :])
+            scaled = dot(p_ref[before], u_ref[j, tile(before), :], MID)
             u_ref[j, tile(i), :] = u
             r_ref[j, tile(before), :] = scaled
             l_ref[j, :, tile(before)] = scaled.T
@@ -278,9 +281,9 @@
             l_ref[j, :, tile(k)] = scaled.T
             d_ref[...] = all_ref[j, tile(j), :] - dot(l_ref[j, :, :depth], u_ref[j, :depth, :])
         own = (lane + k * W == sub + b * COARSE).astype(F32)
-        own = own - dot(y_ref[:, :depth], r_ref[k, :depth, :])
+        own = own - dot(y_ref[:, :depth], r_ref[k, :depth, :], MID)
         y_ref[:, tile(k)] = own
-        z_ref[k] = dot(own, inverse)
+        z_ref[k] = dot(own, inverse, MID)
 
     def near_step(k, carry):
         step(k, False, True)
@@ -300,7 +303,7 @@
     for k in reversed(range(tiles)):
         acc = z_ref[k]
         for j in range(k + 1, tiles):
-            acc = acc - dot(solved[j], l_ref[j, :, k * W : k * W + W])
+            acc = acc - dot(solved[j], l_ref[j, :, k * W : k * W + W], MID)
         solved[k] = acc
         inverse_ref[2 * k] = jnp.where(low, acc, 0.0)
         inverse_ref[2 * k + 1] = jnp.where(low, pltpu.roll(acc, COARSE, 1), 0.0)
@@ -519,10 +522,10 @@
             k_ref[e, rows, :] = part[rows] * mask
         m_ref[e] = jnp.concatenate([local_ref[:, span], gap], axis=1)
     part = stack(local_part(col_ref))
+
+    factor(nb, b, spread, all_ref, inverse_ref, u_ref, r_ref, l_ref, y_ref, zf_ref, p_ref, d_ref)
+
     gather_wait(0)
-
-    factor(nb, b, spread, all_ref, inverse_ref, u_ref, r_ref, l_ref, y_ref, zf_ref, p_ref, d_ref)
-
     u = part + stack(coarse_part(0))
     face = face_start(0, u)
     operate(0, u, face, w_ref)

time: 136 us -> 131 us (0.963)
  Pallas kernels: 133 us -> 128 us
    pallas_call x1, Pallas kernels: 133 us -> 128 us  [body(): pl.pallas_call(functools.partial(whole_kernel, nr, nb), out_shape=jax.Sha...]
where the time goes in v1:
time: 131 us
  Pallas kernels  128 us (98%)
  local copies, waits for them, and re-layouts  1.99 us (2%)
    pallas_call x1, Pallas kernels, body(): pl.pallas_call(functools.partial(whole_kernel, nr, nb), out_shape=jax.Sha...  128 us

profile of v1, /device:TPU:1, one launch (start us, length us, event | category | flops | bytes accessed | tf_op | source)
XLA Modules:
  0.0 131.0 jit_solution(16415142874585729198)
XLA Ops:
  0.6 128.3 %whole.1 = f32[2,8,128]{2,1,0:T(8,128)} custom-call(s32[1,16]{1,0:T(1,128)} %bitcast.15, f32[16,64,64]{2,1,0:T(8,128)} %bitcast.10, f32[1,576]{1,0:T(1,128)} %bitcast.13, f32[576,576]{1,0:T(8,128)} %bitcast.8, f32[576,576]{1,0:T(8,128)} %bitcast.9, s32[96,96]{1,0:T(8,128)} %bitcast.12, s32[4,24]{1,0:T(4,128)} %bitcast.14, f32[64,576]{1,0:T(8,128)} %bitcast.11), custom_call_target="tpu_custom_call" | custom-call | tf_op jit(solution)/shard_map/whole/pallas_call | solution.py:588
  129.0 0.7 fusion
  129.7 0.7 squeeze.7
  130.3 0.7 squeeze.6

commit v2 on v1

--- a/solution.py
+++ b/solution.py
@@ -512,14 +512,8 @@
     spread.second(2)
     if tiles > 4:
         spread.first(4)
-    intact = intact_ref[...].astype(F32)
     for e in range(6):
         span = slice(e * NODES, e * NODES + NODES)
-        part = jnp.concatenate([stiffness_ref[:, span], gap], axis=1)
-        mask = jnp.concatenate([intact, gap[:NODES]], axis=1)
-        for c in range(6):
-            rows = slice(c * NODES, c * NODES + NODES)
-            k_ref[e, rows, :] = part[rows] * mask
         m_ref[e] = jnp.concatenate([local_ref[:, span], gap], axis=1)
     part = stack(local_part(col_ref))
 
@@ -528,12 +522,20 @@
     gather_wait(0)
     u = part + stack(coarse_part(0))
     face = face_start(0, u)
+    intact = jnp.concatenate([intact_ref[...].astype(F32), gap[:NODES]], axis=1)
+    for e in range(6):
+        wide = jnp.concatenate([stiffness_ref[:, e * NODES : e * NODES + NODES], gap], axis=1)
+        for c in range(6):
+            rows = slice(c * NODES, c * NODES + NODES)
+            k_ref[e, rows, :] = wide[rows] * intact
     operate(0, u, face, w_ref)
     w = col_to_row(w_ref)
     p = s = q = sol = None
     dot_old = step_old = None
     for i in range(2):
         gather_start(i + 1, with_dots(reduced(w_ref), res * u, w * u))
+        if i == 0:
+            spread.finish()
         part = local_part(w_ref)
         gather_wait(i + 1)
         total_start(i + 1)
@@ -561,20 +563,20 @@
     gather_start(3, with_dots(jnp.zeros((1, LANES), F32), res * u, w * u))
     gather_wait(3)
     total_start(3)
+    for n in range(4):
+        wait_bytes(gather_ref.at[n, pl.ds(0, nb - 1)], gather_send.at[n])
+    for n in range(1, 3):
+        wait_bytes(total_ref.at[n, pl.ds(0, nr - 1)], total_send.at[n])
+    for n in range(3):
+        for d in range(4):
+            wait_bytes(face_ref.at[n], face_send.at[n, d])
     gamma, delta = total_wait(3)
     ratio = gamma / dot_old
     step_size = gamma / (delta - ratio * gamma / step_old)
     out_ref[0] = sol + step_size * (u + ratio * p)
     out_ref[1] = res - step_size * (w + ratio * s)
 
-    spread.finish()
-    for n in range(4):
-        wait_bytes(gather_ref.at[n, pl.ds(0, nb - 1)], gather_send.at[n])
-    for n in range(1, 4):
-        wait_bytes(total_ref.at[n, pl.ds(0, nr - 1)], total_send.at[n])
-    for n in range(3):
-        for d in range(4):
-            wait_bytes(face_ref.at[n], face_send.at[n, d])
+    wait_bytes(total_ref.at[3, pl.ds(0, nr - 1)], total_send.at[3])
 
 
 VMEM = pl.BlockSpec(memory_space=pltpu.VMEM)

time: 131 us -> 131 us (level)
  no operation moved by 1% of the time
where the time goes in v2:
time: 131 us
  Pallas kernels  128 us (98%)
  local copies, waits for them, and re-layouts  1.99 us (2%)
    pallas_call x1, Pallas kernels, body(): pl.pallas_call(functools.partial(whole_kernel, nr, nb), out_shape=jax.Sha...  128 us

profile of v2, /device:TPU:1, one launch (start us, length us, event | category | flops | bytes accessed | tf_op | source)
XLA Modules:
  0.0 130.8 jit_solution(332895877489983885)
XLA Ops:
  0.6 128.2 %whole.1 = f32[2,8,128]{2,1,0:T(8,128)} custom-call(s32[1,16]{1,0:T(1,128)} %bitcast.15, f32[16,64,64]{2,1,0:T(8,128)} %bitcast.10, f32[1,576]{1,0:T(1,128)} %bitcast.13, f32[576,576]{1,0:T(8,128)} %bitcast.8, f32[576,576]{1,0:T(8,128)} %bitcast.9, s32[96,96]{1,0:T(8,128)} %bitcast.12, s32[4,24]{1,0:T(4,128)} %bitcast.14, f32[64,576]{1,0:T(8,128)} %bitcast.11), custom_call_target="tpu_custom_call" | custom-call | tf_op jit(solution)/shard_map/whole/pallas_call | solution.py:590
  128.8 0.7 fusion
  129.5 0.7 squeeze.7
  130.2 0.7 squeeze.6

commit v3 on v2

--- a/solution.py
+++ b/solution.py
@@ -258,13 +258,13 @@
         if column:
             j = k + 1
 
-            @pl.when(k + 5 < tiles)
+            @pl.when(k + 6 < tiles)
             def _():
-                spread.first(k + 5)
-
-            @pl.when(k + 3 < tiles)
+                spread.first(k + 6)
+
+            @pl.when(k + 4 < tiles)
             def _():
-                spread.second(k + 3)
+                spread.second(k + 4)
 
             v = lax.fori_loop(0, turns - j, plain, v)
             spread.need(j)
@@ -516,6 +516,10 @@
         span = slice(e * NODES, e * NODES + NODES)
         m_ref[e] = jnp.concatenate([local_ref[:, span], gap], axis=1)
     part = stack(local_part(col_ref))
+    if tiles > 3:
+        spread.second(3)
+    if tiles > 5:
+        spread.first(5)
 
     factor(nb, b, spread, all_ref, inverse_ref, u_ref, r_ref, l_ref, y_ref, zf_ref, p_ref, d_ref)
 

time: 131 us -> 134 us (1.023)
  Pallas kernels: 128 us -> 131 us
    pallas_call x1, Pallas kernels: 128 us -> 131 us  [body(): pl.pallas_call(functools.partial(whole_kernel, nr, nb), out_shape=jax.Sha...]
where the time goes in v3:
time: 134 us; the launch traced here: 133 us
  Pallas kernels  131 us (98%)
  local copies, waits for them, and re-layouts  1.99 us (1%)
    pallas_call x1, Pallas kernels, body(): pl.pallas_call(functools.partial(whole_kernel, nr, nb), out_shape=jax.Sha...  131 us

profile of v3, /device:TPU:1, one launch (start us, length us, event | category | flops | bytes accessed | tf_op | source)
XLA Modules:
  0.0 133.4 jit_solution(8749936804447910135)
XLA Ops:
  0.6 130.8 %whole.1 = f32[2,8,128]{2,1,0:T(8,128)} custom-call(s32[1,16]{1,0:T(1,128)} %bitcast.15, f32[16,64,64]{2,1,0:T(8,128)} %bitcast.10, f32[1,576]{1,0:T(1,128)} %bitcast.13, f32[576,576]{1,0:T(8,128)} %bitcast.8, f32[576,576]{1,0:T(8,128)} %bitcast.9, s32[96,96]{1,0:T(8,128)} %bitcast.12, s32[4,24]{1,0:T(4,128)} %bitcast.14, f32[64,576]{1,0:T(8,128)} %bitcast.11), custom_call_target="tpu_custom_call" | custom-call | tf_op jit(solution)/shard_map/whole/pallas_call | solution.py:594
  131.4 0.7 fusion
  132.1 0.7 squeeze.7
  132.8 0.7 squeeze.6
